TPU v7x, 256 devices: a whole 4x4x8 slice. The times are simulated.
256 devices in a mesh: dp: 4 (over y), expert: 8 (over z), tensor: 8 (over x, core).
Axes of the slice: x: 4, y: 4, z: 8, core: 2. Of those that a mesh axis runs over, the one named last changes fastest.
Arguments:
- grad_out: bfloat16 [4096, 6144], P(('dp', 'expert')), may hold values from -1.5 to 1.5
- routes: int32 [4096, 2], P(('dp', 'expert')), may hold values from 0 to 7, as said below
- combine: bfloat16 [4096, 2], P(('dp', 'expert')), may hold values from 0.099609375 to 0.8984375
- saved_hidden: bfloat16 [4, 8, 384, 12288], P(None, 'expert', None, ('dp', 'tensor')), may hold values from -6 to 6
- down_weight: bfloat16 [8, 12288, 6144], P('expert', ('dp', 'tensor')), may hold values from -0.0546875 to 0.0546875
Outputs:
- grad_hidden: bfloat16 [4, 8, 384, 12288], P(None, 'expert', None, ('dp', 'tensor'))
- grad_down: bfloat16 [8, 12288, 6144], P('expert', ('dp', 'tensor'))
- grad_combine: float32 [4096, 2], P(('dp', 'expert'))
Inputs may be any that keep to these rules, and one draw needn't show every extreme that they name: `routes`: the two experts of a token differ. Among the 128 tokens of one group no expert is named more than 48 times, and in every replica one expert is named exactly 48 times by the tokens of each of its groups.
All inputs are finite; a program needn't handle non-finite values.
Results may differ from a plain program's by a relative error of at most 0.0049.
Values may be sent and summed in bfloat16 or wider, within the bound.
No kernel may reach another device: no remote copies, remote signals or barrier semaphores. Data moves between devices by JAX's collectives and lax.ppermute only.
A program may use at most 192 MiB of HBM per device.

v0:
```python
import jax
import jax.numpy as jnp
from jax import lax
from jax.sharding import PartitionSpec as P


def expert_terms(slot_rows, slot_weights, hidden, weight):
    update = lax.dot_general(
        slot_rows, weight, (((1,), (1,)), ((), ())), preferred_element_type=jnp.float32
    )
    scaling = slot_weights.astype(jnp.float32)[:, None]
    grad_rows = (scaling * update).astype(jnp.bfloat16)
    partial_value = jnp.sum(hidden.astype(jnp.float32) * update, axis=1)
    weighted = (scaling * hidden.astype(jnp.float32)).astype(jnp.bfloat16)
    grad_weight = lax.dot_general(
        weighted, slot_rows, (((0,), (0,)), ((), ())), preferred_element_type=jnp.float32
    )
    return (grad_rows, partial_value, grad_weight)


def per_device(grad_out, routes, combine, saved_hidden, down_weight):
    n_expert = lax.axis_size("expert")
    n_tensor = lax.axis_size("tensor")
    n_replica = lax.axis_size("dp")
    tokens_here = grad_out.shape[0]
    most_slots = 3 * tokens_here // n_expert
    share = most_slots // n_tensor
    width = grad_out.shape[1]
    capacity = saved_hidden.shape[2]
    shard_units = saved_hidden.shape[3]
    expert_ids = jnp.arange(n_expert, dtype=jnp.int32)
    hit_table = jnp.sum((routes[:, :, None] == expert_ids).astype(jnp.int32), axis=1)
    before = jnp.cumsum(hit_table, axis=0) - hit_table
    ranking = jnp.take_along_axis(before, routes, axis=1)
    target = routes * most_slots + ranking
    slot_ids = jnp.arange(n_expert * most_slots, dtype=jnp.int32)
    chosen = target[None, :, :] == slot_ids[:, None, None]
    tensor_place = lax.axis_index("tensor")
    picker = (
        jnp.any(chosen, axis=2).astype(jnp.bfloat16).reshape(n_expert, n_tensor, share, tokens_here)
    )
    picker_mine = lax.dynamic_index_in_dim(picker, tensor_place, 1, keepdims=False)
    send_rows = jnp.einsum(
        "esn,nd->esd", picker_mine, grad_out, preferred_element_type=jnp.float32
    ).astype(jnp.bfloat16)
    weight_table = jnp.sum(
        chosen.astype(jnp.float32) * combine.astype(jnp.float32)[None], axis=(1, 2)
    )
    weight_table = weight_table.reshape(n_expert, n_tensor, share)
    send_weights = lax.dynamic_index_in_dim(weight_table, tensor_place, 1, keepdims=False).astype(
        jnp.bfloat16
    )
    recv_rows, recv_weights = (
        lax.all_to_all(send_rows, "expert", split_axis=0, concat_axis=0, tiled=True),
        lax.all_to_all(send_weights, "expert", split_axis=0, concat_axis=0, tiled=True),
    )
    weight = down_weight[0]
    hidden = saved_hidden.reshape(n_replica, n_expert, n_tensor, share, shard_units)
    hidden = hidden.transpose(0, 2, 1, 3, 4).reshape(-1, shard_units)
    all_rows, all_weights = (
        lax.all_gather(recv_rows[None], ("dp", "tensor"), axis=0, tiled=True),
        lax.all_gather(recv_weights[None], ("dp", "tensor"), axis=0, tiled=True),
    )
    grad_slots, partial_value, grad_weight = expert_terms(
        all_rows.reshape(-1, width), all_weights.reshape(-1), hidden, weight
    )
    grad_hidden = grad_slots.reshape(n_replica, n_tensor, n_expert, share, shard_units)
    grad_hidden = grad_hidden.transpose(0, 2, 1, 3, 4).reshape(n_replica, 1, capacity, shard_units)
    grad_down = grad_weight.astype(jnp.bfloat16)[None]
    own_sums = lax.psum_scatter(partial_value, ("dp", "tensor"), scatter_dimension=0, tiled=True)
    returned = lax.all_to_all(
        own_sums.reshape(n_expert, share), "expert", split_axis=0, concat_axis=0, tiled=True
    )
    whole_sums = lax.all_gather(returned[:, None, :], "tensor", axis=1, tiled=True).reshape(-1)
    grad_combine = jnp.sum(chosen.astype(jnp.float32) * whole_sums[:, None, None], axis=0)
    return (grad_hidden, grad_down, grad_combine)


def solution(mesh):
    return jax.shard_map(
        per_device,
        mesh=mesh,
        in_specs=(
            P(("dp", "expert"), None),
            P(("dp", "expert"), None),
            P(("dp", "expert"), None),
            P(None, "expert", None, ("dp", "tensor")),
            P("expert", ("dp", "tensor"), None),
        ),
        out_specs=(
            P(None, "expert", None, ("dp", "tensor")),
            P("expert", ("dp", "tensor"), None),
            P(("dp", "expert"), None),
        ),
        check_vma=False,
    )
```

profile of v0, /device:TPU:1, one launch (start us, length us, event | category | flops | bytes accessed | tf_op | source)
XLA Modules:
  0.0 347.5 jit_solution(7447465027577614276)
XLA Ops:
  7.2 0.8 convert_reduce_fusion
  9.3 1.9 gather_fusion
  12.3 30.4 %all_to_all.20 = bf16[8,6,6144]{2,1,0:T(8,128)(2,1)S(1)} all-to-all(bf16[8,6,6144]{2,1,0:T(8,128)(2,1)S(1)} %copy.105), channel_id=1, replica_groups=mesh['dp'=4,'expert'=8,'tensor'=8] {'expert'}, dimensions={0} | all-to-all | bytes 1179648 | tf_op jit(solution)/shard_map/all_to_all | solution.py:54
  42.7 1.1 copy.106
  43.9 0.9 copy.110
  44.8 1.4 copy-done.2
  46.2 2.1 copy.112
  48.3 4.0 %reshape.75 = f32[1536,384]{1,0:T(8,128)} reshape(f32[4,8,8,6,384]{4,3,2,1,0:T(8,128)} %copy.112) | data formatting | bytes 4718592 | tf_op jit(solution)/shard_map/convert_element_type | solution.py:14
  53.5 71.6 %all-gather.4.cloned.1.call-done = bf16[256,6,6144]{2,0,1:T(8,128)(2,1)} async-done(((bf16[8,6,6144]{2,0,1:T(8,128)(2,1)}), bf16[256,6,6144]{2,0,1:T(8,128)(2,1)}) %all-gather.4.cloned.1.call-update) | async-done | bytes 18874384 | tf_op jit(solution)/shard_map/all_gather | solution.py:61
  125.1 19.8 %copy.107 = bf16[256,6,6144]{2,1,0:T(8,128)(2,1)} copy(bf16[256,6,6144]{2,0,1:T(8,128)(2,1)} %all-gather.4.cloned.1.call-done) | data formatting | bytes 37748736 | tf_op jit(solution)/shard_map/all_gather | solution.py:61
  145.0 27.2 %reshape.70 = bf16[1536,6144]{1,0:T(8,128)(2,1)} reshape(bf16[256,6,6144]{2,1,0:T(8,128)(2,1)} %copy.107) | data formatting | bytes 37748736 | tf_op jit(solution)/shard_map/reshape | solution.py:65
  172.2 16.6 %multiply_reduce_fusion = (f32[1536]{0:T(1024)S(1)}, f32[1536,384]{1,0:T(8,128)}) fusion(f32[1536,384]{1,0:T(8,128)} %reshape.75, bf16[1536,6144]{1,0:T(8,128)(2,1)} %reshape.70, bf16[1,384,6144]{2,1,0:T(8,128)(2,1)} %param.9), kind=kOutput, calls=%fused_computation.6 | convolution fusion | flops 7248935424 | bytes 28317696 | tf_op jit(solution)/shard_map/dot_general | solution.py:8
  188.8 63.2 %all-reduce = f32[1536]{0:T(1024)S(1)} all-reduce(f32[1536]{0:T(1024)S(1)} %get-tuple-element.20), channel_id=4, replica_groups=mesh['dp'=4,'expert'=8,'tensor'=8] {'dp','tensor'}, use_global_device_ids=true, to_apply=%region_5.6.clone | all-reduce | flops 1536 | bytes 12288
  252.8 6.7 %all-to-all-start.2 = ((f32[8,1,6]{2,1,0:T(1,128)}), f32[8,1,6]{2,1,0:T(1,128)S(1)}, u32[]{:S(2)}, u32[]{:S(2)}) async-start(f32[8,1,6]{2,1,0:T(1,128)} %bitcast.11), calls=%async_computation.2 | async-start | bytes 8192 | tf_op jit(solution)/shard_map/all_to_all | solution.py:71
  259.5 6.4 %all-to-all-done.2 = f32[8,1,6]{2,1,0:T(1,128)S(1)} async-done(((f32[8,1,6]{2,1,0:T(1,128)}), f32[8,1,6]{2,1,0:T(1,128)S(1)}, u32[]{:S(2)}, u32[]{:S(2)}) %all-to-all-start.2) | async-done | bytes 224 | tf_op jit(solution)/shard_map/all_to_all | solution.py:71
  266.0 17.5 %all_gather.11 = f32[8,8,6]{2,0,1:T(8,128)S(1)} all-gather(f32[8,1,6]{2,0,1:T(8,128)S(1)} %bitcast.36), channel_id=1, replica_groups=mesh['dp'=4,'expert'=8,'tensor'=8] {'tensor'}, dimensions={1}, use_global_device_ids=true | all-gather | bytes 1728 | tf_op jit(solution)/shard_map/all_gather | solution.py:74
  283.7 0.7 select_reduce_fusion
  284.5 8.9 %all_to_all.21 = bf16[8,1,6]{2,1,0:T(2,128)(2,1)S(1)} all-to-all(bf16[8,1,6]{2,1,0:T(2,128)(2,1)S(1)} %dynamic-slice_convert_fusion), channel_id=1, replica_groups=mesh['dp'=4,'expert'=8,'tensor'=8] {'expert'}, dimensions={0} | all-to-all | bytes 192 | tf_op jit(solution)/shard_map/all_to_all | solution.py:55
  293.4 22.5 %all-gather = bf16[256,1,6]{2,0,1:T(8,128)(2,1)S(1)} all-gather(bf16[8,1,6]{2,0,1:T(8,128)(2,1)S(1)} %copy.103), channel_id=2, replica_groups=mesh['dp'=4,'expert'=8,'tensor'=8] {'dp','tensor'}, dimensions={0}, use_global_device_ids=true | all-gather | bytes 3168 | tf_op jit(solution)/shard_map/all_gather | solution.py:62
  316.1 1.9 multiply_convert_fusion.1
  318.5 1.5 copy.108
  320.1 1.2 copy.116
  321.7 2.2 multiply_convert_fusion
  324.7 15.9 %fusion = bf16[1,384,6144]{2,1,0:T(8,128)(2,1)} fusion(bf16[1536,384]{1,0:T(8,128)(2,1)S(1)} %convert_element_type.75, bf16[1536,6144]{1,0:T(8,128)(2,1)} %reshape.70), kind=kOutput, calls=%fused_computation.2 | convolution fusion | flops 7250116608 | bytes 24772608 | tf_op jit(solution)/shard_map/dot_general | solution.py:15
  (44 shorter events, 5.8 us)
Async XLA Ops:
  7.2 4.4 %copy-start = (bf16[128,6144]{1,0:T(8,128)(2,1)S(1)}, bf16[128,6144]{1,0:T(8,128)(2,1)}, u32[]{:S(2)}) copy-start(bf16[128,6144]{1,0:T(8,128)(2,1)} %param.5) | copy-start | bytes 4718596
  7.2 118.0 %all-gather.4.cloned.1.call-start = ((), (), s32[]{:S(2)}) async-start(), calls=%async_computation.3 | async-start | bytes 19464192 | tf_op jit(solution)/shard_map/all_gather | solution.py:61
  9.3 2.2 copy-start.4
  11.9 32.0 %copy-start.3 = (bf16[4,1,384,384]{3,2,1,0:T(8,128)(2,1)S(1)}, bf16[4,1,384,384]{3,2,1,0:T(8,128)(2,1)}, u32[]{:S(2)}) copy-start(bf16[4,1,384,384]{3,2,1,0:T(8,128)(2,1)} %param.8) | copy-start | bytes 3538948
  44.8 1.4 copy-start.2
  48.3 4.0 %copy-start.6 = (u32[256]{0:T(256)S(1)}, u32[256]{0:T(256)}, u32[]{:S(2)}) copy-start(u32[256]{0:T(256)} %constant.57) | copy-start | bytes 3076
  172.2 87.3 %copy-start.5 = (bf16[128,2]{0,1:T(2,128)(2,1)S(1)}, bf16[128,2]{0,1:T(2,128)(2,1)}, u32[]{:S(2)}) copy-start(bf16[128,2]{0,1:T(2,128)(2,1)} %param.7) | copy-start | bytes 1540
  252.8 13.2 %all-to-all-start.2 = ((f32[8,1,6]{2,1,0:T(1,128)}), f32[8,1,6]{2,1,0:T(1,128)S(1)}, u32[]{:S(2)}, u32[]{:S(2)}) async-start(f32[8,1,6]{2,1,0:T(1,128)} %bitcast.11), calls=%async_computation.2 | async-start | bytes 8192 | tf_op jit(solution)/shard_map/all_to_all | solution.py:71
  324.7 15.9 %copy-start.1 = (bf16[128,6144]{1,0:T(8,128)(2,1)S(1)}, bf16[128,6144]{1,0:T(8,128)(2,1)}, u32[]{:S(2)}) copy-start(bf16[128,6144]{1,0:T(8,128)(2,1)} %param.5) | copy-start | bytes 4718596
Sparse Core Ops, SparseCore 0:
  44.0 81.0 all-gather.3
where the time goes:
time: 349 us; the launch traced here: 347 us
  blocking collectives  143 us (41%)
  waiting for transfers between devices  78.1 us (22%)
  local copies, waits for them, and re-layouts  65.7 us (19%)
  matrix products  32.8 us (9%)
  between operations  14.9 us (4%)
  starting transfers between devices  6.77 us (2%)
  other arithmetic  6.6 us (2%)
    all_gather x1, waiting for transfers between devices, per_device(): lax.all_gather(recv_rows[None], ('dp', 'tensor'), axis=0, tiled=True)  71.6 us
    unnamed x1, blocking collectives  63.2 us
    all_to_all x1, blocking collectives, per_device(): lax.all_to_all(send_rows, 'expert', split_axis=0, concat_axis=0, tiled=True)  30.4 us
    reshape x1, local copies, waits for them, and re-layouts, per_device(): all_rows.reshape(-1, width)  27.2 us
    all_gather x1, blocking collectives, per_device(): lax.all_gather(recv_weights[None], ('dp', 'tensor'), axis=0, tiled=True)  22.5 us
    all_gather x1, local copies, waits for them, and re-layouts, per_device(): lax.all_gather(recv_rows[None], ('dp', 'tensor'), axis=0, tiled=True)  19.8 us
    all_gather x1, blocking collectives, per_device(): lax.all_gather(returned[:, None, :], 'tensor', axis=1, tiled=True)  17.5 us
    dot_general x1, matrix products, expert_terms(): lax.dot_general(slot_rows, weight, (((1,), (1,)), ((), ())), preferred_el...  16.6 us
  transfers between devices with their start and end apart: 2, of which 2 were waited for; matrix products, arithmetic and copies ran while one was open for 2% of the time, Pallas kernels for 0%

commit v1 on v0

v1 whole, which is shorter than its diff:
```python
import jax
import jax.numpy as jnp
from jax import lax
from jax.experimental import pallas as pl
from jax.experimental.pallas import tpu as pltpu
from jax.sharding import PartitionSpec as P

F32, BF16 = jnp.float32, jnp.bfloat16
VMEM_LIMIT = 56 * 1024 * 1024


def slots_of(routes, most):
    tokens = routes.shape[0]
    lanes = lax.broadcasted_iota(jnp.int32, (tokens, 128), 1)
    hits = [routes[:, k : k + 1] == lanes for k in range(2)]
    counts = sum(h.astype(F32) for h in hits).astype(BF16)
    row = lax.broadcasted_iota(jnp.int32, (tokens, tokens), 0)
    col = lax.broadcasted_iota(jnp.int32, (tokens, tokens), 1)
    before = jnp.dot((col < row).astype(F32).astype(BF16), counts, preferred_element_type=F32)
    ranks = [jnp.sum(jnp.where(h, before, 0.0), axis=1, keepdims=True) for h in hits]
    return [
        routes[:, k : k + 1].astype(F32) * float(most) + ranks[k] for k in range(2)
    ]


def pick_kernel(place, routes, combine, grad, out, target):
    slots = out.shape[0]
    tokens = routes.shape[0]
    where = slots_of(routes[...], slots // 8)
    lane = lax.broadcasted_iota(jnp.int32, (tokens, slots), 1).astype(F32)
    weights = combine[...].astype(F32)
    picker = sum(
        jnp.where(where[k] == lane, weights[:, k : k + 1], 0.0) for k in range(2)
    ).astype(BF16)
    rows = lax.dot_general(
        picker, grad[...], (((0,), (0,)), ((), ())), preferred_element_type=F32
    )
    out[...] = rows.astype(BF16)
    target[...] = jnp.concatenate(where, axis=1)


def pick(routes, combine, grad_out, place, n_place, slots):
    tokens, width = grad_out.shape
    cols = width // n_place
    return pl.pallas_call(
        pick_kernel,
        grid_spec=pltpu.PrefetchScalarGridSpec(
            num_scalar_prefetch=1,
            grid=(1,),
            in_specs=[
                pl.BlockSpec((tokens, 2), lambda i, t: (0, 0)),
                pl.BlockSpec((tokens, 2), lambda i, t: (0, 0)),
                pl.BlockSpec((tokens, cols), lambda i, t: (0, t[0])),
            ],
            out_specs=[
                pl.BlockSpec((slots, cols), lambda i, t: (0, 0)),
                pl.BlockSpec((tokens, 2), lambda i, t: (0, 0)),
            ],
        ),
        out_shape=[
            jax.ShapeDtypeStruct((slots, cols), BF16),
            jax.ShapeDtypeStruct((tokens, 2), F32),
        ],
        cost_estimate=pl.CostEstimate(
            flops=2 * tokens * slots * cols, bytes_accessed=4 * slots * cols, transcendentals=0
        ),
    )(place, routes, combine, grad_out)


def update_kernel(first, second, weight, hidden, grad_hidden, partial, acc):
    t = pl.program_id(0)
    n_rep = hidden.shape[0]
    half = first.shape[2]
    capacity = hidden.shape[1]

    @pl.when(t == 0)
    def _():
        acc[...] = jnp.zeros_like(acc)

    for h, ref in enumerate((first, second)):
        for p in range(n_rep):
            acc[p, h * half : (h + 1) * half, :] += lax.dot_general(
                ref[p, 0], weight[...], (((1,), (1,)), ((), ())), preferred_element_type=F32
            )

    @pl.when(t == pl.num_programs(0) - 1)
    def _():
        for p in range(n_rep):
            whole = acc[p]
            grad_hidden[p] = whole.astype(BF16)
            prod = whole * hidden[p].astype(F32)
            folded = sum(prod[:, i : i + 128] for i in range(0, prod.shape[1], 128))
            partial[p : p + 1, :] = jnp.sum(folded.T, axis=0, keepdims=True)


def update(first, second, weight, hidden):
    n_rep, n_place, half, cols = first.shape
    units, width = weight.shape
    capacity = hidden.shape[1]
    block = pl.BlockSpec((n_rep, 1, half, cols), lambda t: (0, t, 0, 0))
    return pl.pallas_call(
        update_kernel,
        grid=(n_place,),
        in_specs=[
            block,
            block,
            pl.BlockSpec((units, cols), lambda t: (0, t)),
            pl.BlockSpec((n_rep, capacity, units), lambda t: (0, 0, 0)),
        ],
        out_specs=[
            pl.BlockSpec((n_rep, capacity, units), lambda t: (0, 0, 0)),
            pl.BlockSpec((n_rep, capacity), lambda t: (0, 0)),
        ],
        out_shape=[
            jax.ShapeDtypeStruct((n_rep, capacity, units), BF16),
            jax.ShapeDtypeStruct((n_rep, capacity), F32),
        ],
        scratch_shapes=[pltpu.VMEM((n_rep, capacity, units), F32)],
        compiler_params=pltpu.CompilerParams(vmem_limit_bytes=VMEM_LIMIT),
        cost_estimate=pl.CostEstimate(
            flops=2 * n_rep * capacity * units * width,
            bytes_accessed=2 * (n_rep * capacity * (width + 2 * units) + units * width),
            transcendentals=0,
        ),
    )(first, second, weight, hidden)


def down_kernel(first, second, turned, out):
    n_rep, _, half, cols = first.shape
    total = None
    for h, ref in enumerate((first, second)):
        for p in range(n_rep):
            term = jnp.dot(
                turned[2 * p + h], ref[p, 0], preferred_element_type=F32
            )
            total = term if total is None else total + term
    out[...] = total.astype(BF16)


def down(first, second, turned):
    n_rep, n_place, half, cols = first.shape
    units = turned.shape[1]
    block = pl.BlockSpec((n_rep, 1, half, cols), lambda t: (0, t, 0, 0))
    return pl.pallas_call(
        down_kernel,
        grid=(n_place,),
        in_specs=[block, block, pl.BlockSpec(turned.shape, lambda t: (0, 0, 0))],
        out_specs=pl.BlockSpec((units, cols), lambda t: (0, t)),
        out_shape=jax.ShapeDtypeStruct((units, n_place * cols), BF16),
        compiler_params=pltpu.CompilerParams(vmem_limit_bytes=VMEM_LIMIT),
        cost_estimate=pl.CostEstimate(
            flops=4 * n_rep * half * units * n_place * cols,
            bytes_accessed=4 * (n_rep * half + units) * n_place * cols,
            transcendentals=0,
        ),
    )(first, second, turned)


def per_device(grad_out, routes, combine, saved_hidden, down_weight):
    n_expert = lax.axis_size("expert")
    n_tensor = lax.axis_size("tensor")
    n_replica = lax.axis_size("dp")
    capacity = saved_hidden.shape[2]
    units = saved_hidden.shape[3]
    most = capacity // n_expert
    half = capacity // 2
    cols = grad_out.shape[1] // n_tensor
    place = lax.axis_index("tensor").astype(jnp.int32).reshape(1)
    rows, target = pick(routes, combine, grad_out, place, n_tensor, capacity)
    got = lax.all_to_all(
        rows.reshape(n_expert, most, cols), "expert", split_axis=0, concat_axis=0, tiled=True
    ).reshape(capacity, cols)
    first, second = (
        lax.all_gather(part, ("dp", "tensor"), axis=0).reshape(n_replica, n_tensor, half, cols)
        for part in (got[:half], got[half:])
    )
    hidden = saved_hidden[:, 0]
    turned = hidden.reshape(2 * n_replica, half, units).transpose(0, 2, 1)
    grad_hidden, partial = update(first, second, down_weight[0], hidden)
    grad_down = down(first, second, turned)
    spread = jnp.broadcast_to(
        partial.reshape(n_replica, n_expert, 1, most), (n_replica, n_expert, n_tensor, most)
    ).reshape(-1, 1, most)
    returned = lax.all_to_all(
        spread, ("dp", "expert", "tensor"), split_axis=0, concat_axis=0, tiled=True
    )
    sums = jnp.sum(returned.reshape(n_replica, n_expert, n_tensor, most), axis=(0, 2)).reshape(-1)
    slot = jnp.arange(capacity, dtype=jnp.int32).astype(F32)
    chosen = target[None] == slot[:, None, None]
    grad_combine = jnp.sum(jnp.where(chosen, sums[:, None, None], 0.0), axis=0) / combine.astype(F32)
    return grad_hidden[:, None], grad_down[None], grad_combine


def solution(mesh):
    return jax.shard_map(
        per_device,
        mesh=mesh,
        in_specs=(
            P(("dp", "expert"), None),
            P(("dp", "expert"), None),
            P(("dp", "expert"), None),
            P(None, "expert", None, ("dp", "tensor")),
            P("expert", ("dp", "tensor"), None),
        ),
        out_specs=(
            P(None, "expert", None, ("dp", "tensor")),
            P("expert", ("dp", "tensor"), None),
            P(("dp", "expert"), None),
        ),
        check_vma=False,
    )
```

time: 349 us -> 217 us (0.62)
  blocking collectives: 143 us -> 26.5 us
  local copies, waits for them, and re-layouts: 65.7 us -> 7.73 us
  waiting for transfers between devices: 78.1 us -> 120 us
  Pallas kernels: 0 us -> 35.9 us
  matrix products: 32.8 us -> 0 us
  other arithmetic: 6.6 us -> 0.78 us
  starting transfers between devices: 6.77 us -> 11.2 us
    unnamed x1 -> x0, blocking collectives: 63.2 us -> none
    all_gather x1 -> x2, waiting for transfers between devices: 71.6 us -> 119 us  [per_device(): lax.all_gather(part, ('dp', 'tensor'), axis=0)]
    all_gather x2 -> x0, blocking collectives: 40.1 us -> none  [the longest x1 22.5 us: per_device(): lax.all_gather(recv_weights[None], ('dp', 'tensor'), axis=0, tiled=True)]
    pallas_call x0 -> x3, Pallas kernels: none -> 35.9 us  [the longest x1 17.6 us: update(): pl.pallas_call(update_kernel, grid=(n_place,), in_specs=[block, block, pl...]
    dot_general x3 -> x0, matrix products: 32.8 us -> none  [the longest x1 16.6 us: expert_terms(): lax.dot_general(slot_rows, weight, (((1,), (1,)), ((), ())), preferred_el...]
    reshape x4 -> x0, local copies, waits for them, and re-layouts: 27.9 us -> none  [the longest x1 27.2 us: per_device(): all_rows.reshape(-1, width)]
    all_gather x2 -> x0, local copies, waits for them, and re-layouts: 19.8 us -> none  [the longest x1 19.8 us: per_device(): lax.all_gather(recv_rows[None], ('dp', 'tensor'), axis=0, tiled=True)]
    all_to_all x2 -> x1, blocking collectives: 39.3 us -> 26.5 us  [per_device(): lax.all_to_all(rows.reshape(n_expert, most, cols), 'expert', split_axis=0...]
  transfers between devices with their start and end apart: 2 -> 3, of which waited for: 2 -> 2; matrix products, arithmetic and copies ran while one was open for 2% -> 1% of each run, Pallas kernels for 0% -> 7%
where the time goes in v1:
time: 217 us; the launch traced here: 216 us
  waiting for transfers between devices  120 us (55%)
  Pallas kernels  35.9 us (17%)
  blocking collectives  26.5 us (12%)
  between operations  14.1 us (6%)
  starting transfers between devices  11.2 us (5%)
  local copies, waits for them, and re-layouts  7.73 us (4%)
    all_gather x2, waiting for transfers between devices, per_device(): lax.all_gather(part, ('dp', 'tensor'), axis=0)  119 us
    all_to_all x1, blocking collectives, per_device(): lax.all_to_all(rows.reshape(n_expert, most, cols), 'expert', split_axis=0...  26.5 us
    pallas_call x1, Pallas kernels, update(): pl.pallas_call(update_kernel, grid=(n_place,), in_specs=[block, block, pl...  17.6 us
    pallas_call x1, Pallas kernels, down(): pl.pallas_call(down_kernel, grid=(n_place,), in_specs=[block, block, pl.B...  15.7 us
    all_to_all x1, starting transfers between devices, per_device(): lax.all_to_all(spread, ('dp', 'expert', 'tensor'), split_axis=0, concat_a...  11.1 us
  transfers between devices with their start and end apart: 3, of which 2 were waited for; matrix products, arithmetic and copies ran while one was open for 1% of the time, Pallas kernels for 7%

profile of v1, /device:TPU:1, one launch (start us, length us, event | category | flops | bytes accessed | tf_op | source)
XLA Modules:
  0.0 215.9 jit_solution(4922565112936066228)
XLA Ops:
  7.2 0.0 copy-start
  7.2 0.0 all-gather.3.cloned.1.call-start
  7.2 1.5 copy.20.combine
  8.7 1.4 copy.19.routes
  10.1 2.6 %shard_map.76 = (bf16[384,768]{1,0:T(8,128)(2,1)}, f32[128,2]{1,0:T(8,128)}) custom-call(s32[1]{0:T(128)} %bitcast.place, s32[128,2]{1,0:T(8,128)} %copy.19.routes, bf16[128,2]{1,0:T(8,128)(2,1)} %copy.20.combine, bf16[128,6144]{1,0:T(8,128)(2,1)} %grad.1), custom_call_target="tpu_custom_call" | custom-call | flops 75497472 | bytes 1179648 | tf_op jit(solution)/shard_map/pallas_call | solution.py:45
  12.6 26.5 %all_to_all.10 = bf16[8,48,768]{2,1,0:T(8,128)(2,1)S(1)} all-to-all(bf16[8,48,768]{2,1,0:T(8,128)(2,1)} %bitcast.21), channel_id=1, replica_groups=mesh['dp'=4,'expert'=8,'tensor'=8] {'expert'}, dimensions={0} | all-to-all | bytes 1179648 | tf_op jit(solution)/shard_map/all_to_all | solution.py:170
  39.1 0.8 fusion
  40.0 0.0 all-gather.3.cloned.1.call-update
  40.0 0.0 all-gather.5.cloned.1.call-start
  40.0 0.7 all-gather.5.cloned.1.call-update
  40.7 0.9 copy.22
  41.6 1.6 copy.21
  43.2 55.8 %all-gather.3.cloned.1.call-done = bf16[32,192,768]{2,1,0:T(8,128)(2,1)} async-done(((bf16[1,192,768]{2,1,0:T(8,128)(2,1)}), bf16[32,192,768]{2,1,0:T(8,128)(2,1)}) %all-gather.3.cloned.1.call-update) | async-done | bytes 9437200 | tf_op jit(solution)/shard_map/all_gather | solution.py:174
  99.1 63.2 %all-gather.5.cloned.1.call-done = bf16[32,192,768]{2,1,0:T(8,128)(2,1)} async-done(((bf16[1,192,768]{2,1,0:T(8,128)(2,1)}), bf16[32,192,768]{2,1,0:T(8,128)(2,1)}) %all-gather.5.cloned.1.call-update) | async-done | bytes 9437200 | tf_op jit(solution)/shard_map/all_gather | solution.py:174
  162.3 17.6 %shard_map.77 = (bf16[4,384,384]{2,1,0:T(8,128)(2,1)}, f32[4,384]{1,0:T(4,128)}) custom-call(bf16[4,8,192,768]{3,2,1,0:T(8,128)(2,1)} %bitcast.23, bf16[4,8,192,768]{3,2,1,0:T(8,128)(2,1)} %bitcast.25, bf16[384,6144]{1,0:T(8,128)(2,1)} %bitcast.27, bf16[4,384,384]{2,1,0:T(8,128)(2,1)} %bitcast.19), custom_call_target="tpu_custom_call" | custom-call | flops 7247757312 | bytes 25952256 | tf_op jit(solution)/shard_map/pallas_call | solution.py:101
  179.9 0.8 broadcast_in_dim.31
  180.7 0.7 broadcast_in_dim.32
  181.3 11.1 %all-to-all-start.1 = ((f32[256,1,48]{2,1,0:T(1,128)}), f32[256,1,48]{2,1,0:T(1,128)S(1)}, u32[]{:S(2)}, u32[]{:S(2)}) async-start(f32[256,1,48]{2,1,0:T(1,128)} %bitcast.13), calls=%async_computation.1 | async-start | bytes 262144 | tf_op jit(solution)/shard_map/all_to_all | solution.py:184
  192.4 0.0 copy-start.1
  192.4 15.7 %shard_map.78 = bf16[384,6144]{1,0:T(8,128)(2,1)} custom-call(bf16[4,8,192,768]{3,2,1,0:T(8,128)(2,1)} %bitcast.24, bf16[4,8,192,768]{3,2,1,0:T(8,128)(2,1)} %bitcast.26, bf16[8,384,192]{2,1,0:T(8,128)(2,1)} %bitcast.16), custom_call_target="tpu_custom_call" | custom-call | flops 7247757312 | bytes 28311552 | tf_op jit(solution)/shard_map/pallas_call | solution.py:144
  208.2 0.0 all-to-all-done.1
  208.2 0.1 broadcast_in_dim.33
  208.3 0.2 select_reduce_fusion
  208.5 0.6 convert_divide_fusion
  (4 shorter events, 0.0 us)
Async XLA Ops:
  7.2 34.5 %copy-start = (bf16[4,1,384,384]{3,2,1,0:T(8,128)(2,1)S(1)}, bf16[4,1,384,384]{3,2,1,0:T(8,128)(2,1)}, u32[]{:S(2)}) copy-start(bf16[4,1,384,384]{3,2,1,0:T(8,128)(2,1)} %param.8) | copy-start | bytes 3538948
  7.2 91.9 %all-gather.3.cloned.1.call-start = ((), (), s32[]{:S(2)}) async-start(), calls=%async_computation.2 | async-start | bytes 9732096 | tf_op jit(solution)/shard_map/all_gather | solution.py:174
  40.0 122.3 %all-gather.5.cloned.1.call-start = ((), (), s32[]{:S(2)}) async-start(), calls=%async_computation.3 | async-start | bytes 9732096 | tf_op jit(solution)/shard_map/all_gather | solution.py:174
  181.3 26.8 %all-to-all-start.1 = ((f32[256,1,48]{2,1,0:T(1,128)}), f32[256,1,48]{2,1,0:T(1,128)S(1)}, u32[]{:S(2)}, u32[]{:S(2)}) async-start(f32[256,1,48]{2,1,0:T(1,128)} %bitcast.13), calls=%async_computation.1 | async-start | bytes 262144 | tf_op jit(solution)/shard_map/all_to_all | solution.py:184
  192.4 16.0 %copy-start.1 = (bf16[128,2]{0,1:T(2,128)(2,1)S(1)}, bf16[128,2]{0,1:T(2,128)(2,1)}, u32[]{:S(2)}) copy-start(bf16[128,2]{0,1:T(2,128)(2,1)} %param.7) | copy-start | bytes 1540
Sparse Core Ops, SparseCore 0:
  40.1 58.9 all-gather.2
  102.2 60.0 all-gather.4
